TPU v7x, 128 devices: a whole 4x4x4 slice. The times are simulated.
128 devices in a mesh: dp: 8 (over x_lo, z), expert: 16 (over y, x_hi, core).
Axes of the slice: x: 4 (x_hi: 2, x_lo: 2; x = x_hi * 2 + x_lo), y: 4, z: 4, core: 2. Of those that a mesh axis runs over, the one named last changes fastest.
Arguments:
- tokens: bfloat16 [2048, 128, 1280], P(('dp', 'expert')), may hold values from -16 to 16
- slot_params: bfloat16 [1280, 16], replicated, may hold values from -1 to 1
- grad_out: bfloat16 [2048, 128, 1280], P(('dp', 'expert')), may hold values from -6 to 6
- slot_codes: int32 [2048, 16, 1280], P('dp', 'expert'), may hold values from 0 to 254, as said below
- scale_exps: int32 [2048, 16, 10], P('dp', 'expert'), may hold values from -9 to -7
- w_in: bfloat16 [16, 1280, 5120], P('expert', None, 'dp'), may hold values from -0.15625 to 0.15625
- w_out: bfloat16 [16, 5120, 1280], P('expert', 'dp'), may hold values from -0.078125 to 0.078125
Outputs:
- grad_tokens: bfloat16 [2048, 128, 1280], P(('dp', 'expert'))
- grad_params: float32 [1280, 16], replicated
- grad_w_in: bfloat16 [16, 1280, 5120], P('expert', None, 'dp')
- grad_w_out: bfloat16 [16, 5120, 1280], P('expert', 'dp')
Inputs may be any that keep to these rules, and one draw needn't show every extreme that they name: `slot_codes`: codes 127 and 255 never occur.
All inputs are finite; a program needn't handle non-finite values.
Results may differ from a plain program's by a relative error of at most 0.015.
Values may be sent and summed in bfloat16 or wider, within the bound.
A program may use at most 192 MiB of HBM per device.

v0:
```python
import jax
import jax.numpy as jnp
from jax import lax
from jax.sharding import PartitionSpec as P

gelu_coef = 0.7978845608028654


def gelu_both(pre_act):
    inner_arg = gelu_coef * (pre_act + 0.044715 * pre_act * pre_act * pre_act)
    tanh_val = jnp.tanh(inner_arg)
    active = 0.5 * pre_act * (1.0 + tanh_val)
    slope = 0.5 * (1.0 + tanh_val) + 0.5 * pre_act * (1.0 - tanh_val * tanh_val) * gelu_coef * (
        1.0 + 3.0 * 0.044715 * pre_act * pre_act
    )
    return (active, slope)


def decode_slots(slot_codes, exponents, block_len):
    sign_bit = slot_codes // 128
    exponent = slot_codes // 8 % 16
    mantissa = (slot_codes % 8).astype(jnp.float32)
    normal_mag = (1.0 + mantissa / 8.0) * jnp.exp2((exponent - 7).astype(jnp.float32))
    small_mag = mantissa / 8.0 * (1.0 / 64.0)
    magnitude = jnp.where(exponent == 0, small_mag, normal_mag)
    decoded = (1.0 - 2.0 * sign_bit.astype(jnp.float32)) * magnitude
    full_shape = slot_codes.shape
    blocks = decoded.reshape(full_shape[:-1] + (full_shape[-1] // block_len, block_len))
    scaled = blocks * jnp.exp2(exponents.astype(jnp.float32))[..., None]
    return scaled.reshape(full_shape).astype(jnp.bfloat16)


def local(tokens, slot_params, grad_out, slot_codes, scale_exps, w_in, w_out):
    f_type = jnp.float32
    logits = jnp.einsum("bmd,ds->bsm", tokens, slot_params, preferred_element_type=f_type)
    dispatch = jax.nn.softmax(logits, axis=2)
    combine = jax.nn.softmax(logits, axis=1)
    comb_bf = combine.astype(jnp.bfloat16)
    slot_grad = jnp.einsum("bsm,bmd->bsd", comb_bf, grad_out, preferred_element_type=f_type).astype(
        jnp.bfloat16
    )
    recv_grad = lax.all_to_all(slot_grad, "expert", split_axis=1, concat_axis=0, tiled=True)
    block_len = slot_codes.shape[2] // scale_exps.shape[2]
    slot_in = decode_slots(slot_codes, scale_exps, block_len)
    all_in, all_grad = (
        lax.all_gather(slot_in, "dp", axis=0, tiled=True),
        lax.all_gather(recv_grad, "dp", axis=0, tiled=True),
    )
    shard_pre = jnp.einsum("gsd,sdf->gsf", all_in, w_in, preferred_element_type=f_type)
    shard_active, shard_slope = gelu_both(shard_pre)
    shard_hidden = shard_active.astype(jnp.bfloat16)
    shard_hgrad = jnp.einsum("gsd,sfd->gsf", all_grad, w_out, preferred_element_type=f_type)
    shard_pgrad = (shard_hgrad * shard_slope).astype(jnp.bfloat16)
    grad_w_out = jnp.einsum(
        "gsf,gsd->sfd", shard_hidden, all_grad, preferred_element_type=f_type
    ).astype(jnp.bfloat16)
    grad_w_in = jnp.einsum(
        "gsd,gsf->sdf", all_in, shard_pgrad, preferred_element_type=f_type
    ).astype(jnp.bfloat16)
    full_in, full_out = (
        lax.all_gather(w_in, "dp", axis=2, tiled=True),
        lax.all_gather(w_out, "dp", axis=1, tiled=True),
    )
    pre_act = jnp.einsum("gsd,sdf->gsf", slot_in, full_in, preferred_element_type=f_type)
    active, slope = gelu_both(pre_act)
    hidden = active.astype(jnp.bfloat16)
    slot_out = jnp.einsum("gsf,sfd->gsd", hidden, full_out, preferred_element_type=f_type).astype(
        jnp.bfloat16
    )
    hidden_grad = jnp.einsum("gsd,sfd->gsf", recv_grad, full_out, preferred_element_type=f_type)
    pre_grad = (hidden_grad * slope).astype(jnp.bfloat16)
    slot_in_grad = jnp.einsum(
        "gsf,sdf->gsd", pre_grad, full_in, preferred_element_type=f_type
    ).astype(jnp.bfloat16)
    back_out, back_grad = (
        lax.all_to_all(slot_out, "expert", split_axis=0, concat_axis=1, tiled=True),
        lax.all_to_all(slot_in_grad, "expert", split_axis=0, concat_axis=1, tiled=True),
    )
    comb_grad = jnp.einsum("bmd,bsd->bsm", grad_out, back_out, preferred_element_type=f_type)
    logit_comb = combine * (comb_grad - jnp.sum(combine * comb_grad, axis=1, keepdims=True))
    disp_grad = jnp.einsum("bmd,bsd->bsm", tokens, back_grad, preferred_element_type=f_type)
    logit_disp = dispatch * (disp_grad - jnp.sum(dispatch * disp_grad, axis=2, keepdims=True))
    logit_grad = (logit_comb + logit_disp).astype(jnp.bfloat16)
    disp_bf = dispatch.astype(jnp.bfloat16)
    through_slots = jnp.einsum("bsm,bsd->bmd", disp_bf, back_grad, preferred_element_type=f_type)
    through_logits = jnp.einsum(
        "bsm,ds->bmd", logit_grad, slot_params, preferred_element_type=f_type
    )
    grad_tokens = (through_slots + through_logits).astype(jnp.bfloat16)
    local_params = jnp.einsum("bmd,bsm->ds", tokens, logit_grad, preferred_element_type=f_type)
    grad_params = lax.psum(local_params, ("dp", "expert"))
    return (grad_tokens, grad_params, grad_w_in, grad_w_out)


def solution(mesh):
    in_specs = (
        P(("dp", "expert"), None, None),
        P(),
        P(("dp", "expert"), None, None),
        P("dp", "expert", None),
        P("dp", "expert", None),
        P("expert", None, "dp"),
        P("expert", "dp", None),
    )
    out_specs = (
        P(("dp", "expert"), None, None),
        P(),
        P("expert", None, "dp"),
        P("expert", "dp", None),
    )
    return jax.shard_map(local, mesh=mesh, in_specs=in_specs, out_specs=out_specs, check_vma=False)
```

profile of v0, /device:TPU:1, one launch (start us, length us, event | category | flops | bytes accessed | tf_op | source)
XLA Modules:
  0.0 651.8 jit_solution(10657131776974840816)
XLA Ops:
  7.2 0.0 copy-start
  7.2 0.0 all-gather.9.cloned.1.call-start
  7.2 0.7 multiply_exponential_fusion
  8.0 2.5 copy.30
  10.5 0.1 mul.151
  10.6 3.7 fusion.115
  14.2 0.0 all-gather.9.cloned.1.call-update
  14.2 0.0 all-gather.11.cloned.1.call-start
  14.3 0.0 copy-done
  14.3 3.9 convolution_bitcast_fusion.1
  18.2 0.7 fusion.173
  19.0 0.0 copy-start.3
  19.0 3.4 convolution_convert_fusion
  22.4 0.2 copy.29
  22.6 24.6 %all_to_all.54 = bf16[16,16,1280]{2,0,1:T(8,128)(2,1)} all-to-all(bf16[16,16,1280]{2,0,1:T(8,128)(2,1)S(1)} %copy.29), channel_id=1, replica_groups=mesh['dp'=8,'expert'=16] {'expert'}, dimensions={1} | all-to-all | bytes 1310720 | tf_op jit(solution)/shard_map/all_to_all | solution.py:42
  47.2 0.0 all-gather.11.cloned.1.call-update
  47.2 0.0 all-gather.7.cloned.1.call-start
  47.3 0.7 all-gather.7.cloned.1.call-update
  47.9 0.5 all-gather.5.cloned.1.call-start
  48.5 0.1 all-gather.5.cloned.1.call-update
  48.5 0.8 fusion.174
  49.3 42.6 %all-gather.9.cloned.1.call-done = bf16[2048,1,1280]{0,2,1:T(8,128)(2,1)} async-done(((bf16[256,1,1280]{0,2,1:T(8,128)(2,1)}), bf16[2048,1,1280]{0,2,1:T(8,128)(2,1)}) %all-gather.9.cloned.1.call-update) | async-done | bytes 5242896 | tf_op jit(solution)/shard_map/all_gather | solution.py:46
  91.9 0.0 copy-done.3
  91.9 9.1 %fusion.47 = f32[2048,640]{1,0:T(8,128)} fusion(bf16[2048,1,1280]{0,2,1:T(8,128)(2,1)} %all-gather.9.cloned.1.call-done, bf16[1,1280,640]{2,1,0:T(8,128)(2,1)S(1)} %copy-done.3), kind=kOutput, calls=%fused_computation.41 | convolution fusion | flops 3355443200 | bytes 12124160 | tf_op jit(solution)/shard_map/gsd,sdf->gsf/dot_general | solution.py:49
  101.0 0.0 copy-start.1
  101.0 58.3 %all-gather.11.cloned.1.call-done = bf16[2048,1,1280]{2,0,1:T(8,128)(2,1)} async-done(((bf16[256,1,1280]{2,0,1:T(8,128)(2,1)}), bf16[2048,1,1280]{2,0,1:T(8,128)(2,1)}) %all-gather.11.cloned.1.call-update) | async-done | bytes 5242896 | tf_op jit(solution)/shard_map/all_gather | solution.py:47
  159.3 16.9 %fusion.66 = bf16[1,1280,640]{2,1,0:T(8,128)(2,1)} fusion(bf16[2048,1,1280]{0,2,1:T(8,128)(2,1)} %all-gather.9.cloned.1.call-done, f32[2048,640]{1,0:T(8,128)} %fusion.47, bf16[2048,1,1280]{2,0,1:T(8,128)(2,1)} %all-gather.11.cloned.1.call-done, bf16[1,640,1280]{2,1,0:T(8,128)(2,1)} %param.13), kind=kOutput, calls=%fused_computation.55 | convolution fusion | flops 6736609280 | bytes 19005440 | tf_op jit(solution)/shard_map/gsd,gsf->sdf/dot_general | solution.py:57
  176.2 0.0 copy-start.2
  176.2 119.8 %all-gather.7.cloned.1.call-done = bf16[1,1280,5120]{2,1,0:T(8,128)(2,1)} async-done(((bf16[1,1280,640]{2,1,0:T(8,128)(2,1)}), bf16[1,1280,5120]{2,1,0:T(8,128)(2,1)}) %all-gather.7.cloned.1.call-update) | async-done | bytes 13107216 | tf_op jit(solution)/shard_map/all_gather | solution.py:61
  295.9 0.0 copy-done.1
  295.9 10.1 %fusion.18 = f32[256,1,5120]{2,0,1:T(8,128)} fusion(bf16[1,1280,5120]{2,1,0:T(8,128)(2,1)} %all-gather.7.cloned.1.call-done, bf16[256,1,1280]{0,2,1:T(8,128)(2,1)S(1)} %copy-done.1), kind=kOutput, calls=%fused_computation.19 | convolution fusion | flops 3355443200 | bytes 19005440 | tf_op jit(solution)/shard_map/gsd,sdf->gsf/dot_general | solution.py:64
  306.0 126.4 %all-gather.5.cloned.1.call-done = bf16[1,5120,1280]{2,1,0:T(8,128)(2,1)} async-done(((bf16[1,640,1280]{2,1,0:T(8,128)(2,1)}), bf16[1,5120,1280]{2,1,0:T(8,128)(2,1)}) %all-gather.5.cloned.1.call-update) | async-done | bytes 13107216 | tf_op jit(solution)/shard_map/all_gather | solution.py:62
  432.5 0.0 copy-done.2
  432.5 14.4 %fusion.102 = bf16[256,1,1280]{2,0,1:T(8,128)(2,1)S(1)} fusion(bf16[1,1280,5120]{2,1,0:T(8,128)(2,1)} %all-gather.7.cloned.1.call-done, bf16[256,1280]{1,0:T(8,128)(2,1)S(1)} %bitcast.216, bf16[1,5120,1280]{2,1,0:T(8,128)(2,1)} %all-gather.5.cloned.1.call-done, f32[256,1,5120]{2,0,1:T(8,128)} %fusion.18), kind=kOutput, calls=%fused_computation.74 | convolution fusion | flops 6736117760 | bytes 32768000 | tf_op jit(solution)/shard_map/gsf,sdf->gsd/dot_general | solution.py:72
  446.8 0.5 broadcast.141
  447.4 1.1 reduce.1
  448.5 1.0 reshape.96
  449.5 7.1 %all-to-all-start.1 = ((bf16[16,2,10240]{2,1,0:T(2,128)(2,1)}), bf16[16,2,10240]{2,1,0:T(2,128)(2,1)S(1)}, u32[]{:S(2)}, u32[]{:S(2)}) async-start(bf16[16,2,10240]{2,1,0:T(2,128)(2,1)} %reshape.96), calls=%async_computation.1 | async-start | bytes 1310720 | tf_op jit(solution)/shard_map/all_to_all | solution.py:77
  456.6 10.8 %fusion.97 = bf16[256,1,1280]{2,0,1:T(8,128)(2,1)S(1)} fusion(bf16[1,5120,1280]{2,1,0:T(8,128)(2,1)} %all-gather.5.cloned.1.call-done, f32[256,1,5120]{2,0,1:T(8,128)} %fusion.18), kind=kOutput, calls=%fused_computation.73 | convolution fusion | flops 3367567360 | bytes 19005440 | tf_op jit(solution)/shard_map/gsf,sfd->gsd/dot_general | solution.py:67
  467.4 1.1 reduce
  468.5 1.0 reshape.94
  469.5 0.0 all-to-all-done.1
  469.5 7.2 %all-to-all-start.2 = ((bf16[16,2,10240]{2,1,0:T(2,128)(2,1)}), bf16[16,2,10240]{2,1,0:T(2,128)(2,1)S(1)}, u32[]{:S(2)}, u32[]{:S(2)}) async-start(bf16[16,2,10240]{2,1,0:T(2,128)(2,1)} %reshape.94), calls=%async_computation.2 | async-start | bytes 1310720 | tf_op jit(solution)/shard_map/all_to_all | solution.py:76
  476.7 0.2 all-reduce.2.cloned.1.call-start
  477.0 9.4 %fusion.63 = bf16[1,640,1280]{2,1,0:T(8,128)(2,1)} fusion(bf16[2048,1,1280]{2,0,1:T(8,128)(2,1)} %all-gather.11.cloned.1.call-done, f32[2048,640]{1,0:T(8,128)} %fusion.47), kind=kOutput, calls=%fused_computation.54 | convolution fusion | flops 3368058880 | bytes 12124160 | tf_op jit(solution)/shard_map/gsf,gsd->sfd/dot_general | solution.py:54
  486.4 0.6 reshape.97
  487.0 0.1 copy.39
  487.1 3.9 fusion.137
  491.0 0.0 copy-start.5
  491.0 0.0 copy-start.4
  491.0 0.0 all-to-all-done.2
  491.0 0.7 reshape.95
  491.7 0.1 copy.40
  491.8 3.9 fusion.135
  495.7 0.0 copy-done.5
  495.7 0.4 fusion.132
  496.1 0.0 copy-done.4
  496.2 6.0 fusion.134
  502.1 4.1 convolution_bitcast_fusion
  506.2 0.0 all-reduce.2.cloned.1.call-update
  506.2 7.1 %add_convert_fusion = bf16[16,128,1280]{2,1,0:T(8,128)(2,1)} fusion(f32[16,128,1280]{2,1,0:T(8,128)} %fusion.134, bf16[16,16,1,1280]{3,1,0,2:T(8,128)(2,1)S(1)} %bitcast.213, f32[16,16]{1,0:T(8,128)S(1)} %get-tuple-element.6, f32[16,16,128]{2,1,0:T(8,128)S(1)} %convolution_bitcast_fusion.1), kind=kOutput, calls=%fused_computation.12 | convolution fusion | flops 89227648 | bytes 16516096 | tf_op jit(solution)/shard_map/bsm,bsd->bmd/dot_general | solution.py:85
  513.3 130.2 %all-reduce.2.cloned.1.call-done = f32[1280,16]{0,1:T(8,128)} async-done(((f32[1280,16]{0,1:T(8,128)}), f32[1280,16]{0,1:T(8,128)}) %all-reduce.2.cloned.1.call-update) | async-done | bytes 81936 | tf_op jit(solution)/shard_map/psum | solution.py:91
  643.5 1.5 copy.58
  (1 shorter events, 0.0 us)
Async XLA Ops:
  7.2 7.1 %copy-start = (bf16[1280,16]{0,1:T(8,128)(2,1)S(1)}, bf16[1280,16]{0,1:T(8,128)(2,1)}, u32[]{:S(2)}) copy-start(bf16[1280,16]{0,1:T(8,128)(2,1)} %param.8) | copy-start | bytes 122884
  7.2 84.7 %all-gather.9.cloned.1.call-start = ((), (), s32[]{:S(2)}) async-start(), calls=%async_computation.6 | async-start | bytes 5898240 | tf_op jit(solution)/shard_map/all_gather | solution.py:46
  14.2 145.0 %all-gather.11.cloned.1.call-start = ((), (), s32[]{:S(2)}) async-start(), calls=%async_computation.7 | async-start | bytes 5898240 | tf_op jit(solution)/shard_map/all_gather | solution.py:47
  19.0 72.9 %copy-start.3 = (bf16[1,1280,640]{2,1,0:T(8,128)(2,1)S(1)}, bf16[1,1280,640]{2,1,0:T(8,128)(2,1)}, u32[]{:S(2)}) copy-start(bf16[1,1280,640]{2,1,0:T(8,128)(2,1)} %param.12) | copy-start | bytes 4915204
  47.2 248.7 %all-gather.7.cloned.1.call-start = ((), (), s32[]{:S(2)}) async-start(), calls=%async_computation.4 | async-start | bytes 14745600 | tf_op jit(solution)/shard_map/all_gather | solution.py:61
  47.9 384.5 %all-gather.5.cloned.1.call-start = ((), (), s32[]{:S(2)}) async-start(), calls=%async_computation.3 | async-start | bytes 14745600 | tf_op jit(solution)/shard_map/all_gather | solution.py:62
  101.0 195.0 %copy-start.1 = (bf16[256,1,1280]{0,2,1:T(8,128)(2,1)S(1)}, bf16[256,1,1280]{0,2,1:T(8,128)(2,1)}, u32[]{:S(2)}) copy-start(bf16[256,1,1280]{0,2,1:T(8,128)(2,1)} %fusion.115) | copy-start | bytes 1966084
  176.2 256.3 %copy-start.2 = (bf16[16,16,1280]{2,0,1:T(8,128)(2,1)S(1)}, bf16[16,16,1280]{2,0,1:T(8,128)(2,1)}, u32[]{:S(2)}) copy-start(bf16[16,16,1280]{2,0,1:T(8,128)(2,1)} %all_to_all.54) | copy-start | bytes 1966084
  449.5 20.0 %all-to-all-start.1 = ((bf16[16,2,10240]{2,1,0:T(2,128)(2,1)}), bf16[16,2,10240]{2,1,0:T(2,128)(2,1)S(1)}, u32[]{:S(2)}, u32[]{:S(2)}) async-start(bf16[16,2,10240]{2,1,0:T(2,128)(2,1)} %reshape.96), calls=%async_computation.1 | async-start | bytes 1310720 | tf_op jit(solution)/shard_map/all_to_all | solution.py:77
  469.5 21.6 %all-to-all-start.2 = ((bf16[16,2,10240]{2,1,0:T(2,128)(2,1)}), bf16[16,2,10240]{2,1,0:T(2,128)(2,1)S(1)}, u32[]{:S(2)}, u32[]{:S(2)}) async-start(bf16[16,2,10240]{2,1,0:T(2,128)(2,1)} %reshape.94), calls=%async_computation.2 | async-start | bytes 1310720 | tf_op jit(solution)/shard_map/all_to_all | solution.py:76
  476.7 166.8 %all-reduce.2.cloned.1.call-start = ((), (), s32[]{:S(2)}) async-start(), calls=%async_computation.5 | async-start | bytes 163840 | tf_op jit(solution)/shard_map/psum | solution.py:91
  491.0 4.7 copy-start.5
  491.0 5.1 copy-start.4
Sparse Core Ops, SparseCore 0:
  14.4 77.4 all-gather.8
  93.5 65.6 all-gather.10
  160.9 134.9 all-gather.6
  297.4 134.9 all-gather.4
  506.4 137.0 all-reduce.1
where the time goes:
time: 657 us; the launch traced here: 652 us
  waiting for transfers between devices  478 us (73%)
  matrix products  103 us (16%)
  blocking collectives  24.6 us (4%)
  starting transfers between devices  15.2 us (2%)
  between operations  14.1 us (2%)
  other arithmetic  8.5 us (1%)
  local copies, waits for them, and re-layouts  8.27 us (1%)
    psum x1, waiting for transfers between devices, local(): grad_params = lax.psum(local_params, ('dp', 'expert'))  130 us
    all_gather x1, waiting for transfers between devices, local(): lax.all_gather(w_out, 'dp', axis=1, tiled=True)  126 us
    all_gather x1, waiting for transfers between devices, local(): lax.all_gather(w_in, 'dp', axis=2, tiled=True)  120 us
    all_gather x1, waiting for transfers between devices, local(): lax.all_gather(recv_grad, 'dp', axis=0, tiled=True)  58.3 us
    all_gather x1, waiting for transfers between devices, local(): lax.all_gather(slot_in, 'dp', axis=0, tiled=True)  42.6 us
    all_to_all x1, blocking collectives, local(): lax.all_to_all(slot_grad, 'expert', split_axis=1, concat_axis=0, tiled=True)  24.6 us
    dot_general x1, matrix products, local(): jnp.einsum('gsd,gsf->sdf', all_in, shard_pgrad, preferred_element_type=f_...  16.9 us
    dot_general x1, matrix products, local(): jnp.einsum('gsf,sdf->gsd', pre_grad, full_in, preferred_element_type=f_type)  14.4 us
  transfers between devices with their start and end apart: 7, of which 5 were waited for; matrix products, arithmetic and copies ran while one was open for 12% of the time, Pallas kernels for 0%

commit v1 on v0

v1 whole, which is shorter than its diff:
```python
import jax
import jax.numpy as jnp
from jax import lax
from jax.experimental import pallas as pl
from jax.experimental.pallas import tpu as pltpu
from jax.sharding import PartitionSpec as P

F32 = jnp.float32
BF16 = jnp.bfloat16
MESH = pl.DeviceIdType.MESH
gelu_coef = 0.7978845608028654

D, FU = 1280, 640
IMG, PAT, S = 16, 128, 16
ROWS, UNIT = 1024, 128
ND, NE = 8, 16

X1, D1, G2, D2, M1, M2, G1, X2 = range(8)

W_IN, W_OUT = 0, 1
IN_HOP, GR_HOP, OUT_RS, IG_RS = 2, 8, 14, 18
GWO, GWI = 22, 27
A2A_G, A2A_O, A2A_I = 32, 33, 34
GP_A, GP_B, GP_C = 35, 36, 37
N_SEM = 38
L_CODE, L_WIN, L_WOUT, L_TOK, L_GO, L_GT, L_GWO, L_GWI, L_GP = 0, 1, 2, 3, 7, 11, 15, 20, 25
N_LOC = 26


def dot(a, b, ca, cb):
    return lax.dot_general(a, b, (((ca,), (cb,)), ((), ())), preferred_element_type=F32)


def gelu_both(x):
    x2 = x * x
    t = jnp.tanh(gelu_coef * (x + 0.044715 * x * x2))
    h = 0.5 * (1.0 + t)
    return x * h, h + 0.5 * x * (1.0 - t * t) * (gelu_coef + (gelu_coef * 3.0 * 0.044715) * x2)


def unit(u, n=1):
    return pl.ds(u * UNIT, n * UNIT)


def put(ref, rows, value):
    for j in range(D // 128):
        ref[j, rows, :] = value[:, j * 128 : (j + 1) * 128]


def every_16th(ref, start):
    return jnp.concatenate([ref[j, pl.ds(start, 16, stride=16), :].astype(BF16) for j in range(D // 128)], axis=1)


def kernel(
    codes, scales, tokens, gout, par_t, w_in, w_out,
    gt_out, gp_out, gwi_out, gwo_out,
    code_v, tok, go, win, wout, rin, rgr, hid, slope, pg,
    comb, disp, fbuf, gbuf, sg_send, back_o, back_i,
    ps_o, ps_i, kp_o, kp_i, rs_o, rs_i, h2_o, h2_i, fin_o, fin_i,
    gwo_s, gwi_s, gwo_r, gwi_r, gp_acc, gp_s, gp_r1, gp_m, gp_r2, gp_f,
    s_sem, r_sem, l_sem,
):
    d, e = lax.axis_index("dp"), lax.axis_index("expert")
    xl, z, core = d // 4, lax.rem(d, 4), lax.rem(e, 2)
    z_near = z + 1 - 2 * lax.rem(z, 2)
    z_far = 3 - z
    z_pair = z_near * (1 - core) + z_far * core
    z_group = z_far * (1 - core) + z_near * core
    dev_x = ((1 - xl) * 4 + z, e)
    dev_p = (xl * 4 + z_pair, e)
    dev_g = (xl * 4 + z_group, e)
    others_e = [(d, lax.rem(e + k, NE)) for k in range(1, NE)]
    others_d = [(lax.rem(d + k, ND), e) for k in range(1, ND)]

    def remote(src, dst, i, dev):
        return pltpu.make_async_remote_copy(
            src_ref=src, dst_ref=dst, send_sem=s_sem.at[i], recv_sem=r_sem.at[i], device_id=dev, device_id_type=MESH
        )

    def here(src, dst, i):
        return pltpu.make_async_copy(src, dst, l_sem.at[i])

    cp_code = here(codes, code_v, L_CODE)
    cp_win = here(w_in.at[0], win.at[0], L_WIN)
    cp_wout = here(w_out.at[0], wout.at[0], L_WOUT)
    cp_code.start()

    def tok_copy(c):
        return here(tokens.at[pl.ds(c * 4, 4)], tok.at[pl.ds(c * 4, 4)], L_TOK + c)

    def go_copy(c):
        return here(gout.at[pl.ds(c * 4, 4)], go.at[pl.ds(c * 4, 4)], L_GO + c)

    for c in range(4):
        tok_copy(c).start()
        go_copy(c).start()
    cp_win.start()
    cp_wout.start()

    barrier = pltpu.get_barrier_semaphore()
    for dev in others_e + others_d:
        pl.semaphore_signal(barrier, inc=1, device_id=dev, device_id_type=MESH)
    pl.semaphore_wait(barrier, NE + ND - 2)

    c_win = remote(w_in.at[0], win.at[1], W_IN, dev_p)
    c_wout = remote(w_out.at[0], wout.at[1], W_OUT, dev_p)
    c_win.start()

    def row_hops(buf, base):
        first = [
            remote(buf.at[unit(M1)], buf.at[unit(X1)], base, dev_x),
            remote(buf.at[unit(M2)], buf.at[unit(G2)], base + 1, dev_g),
            remote(buf.at[unit(M2)], buf.at[unit(X2)], base + 2, dev_x),
            remote(buf.at[unit(M1)], buf.at[unit(G1)], base + 3, dev_g),
        ]
        second = [
            remote(buf.at[unit(X1)], buf.at[unit(D1)], base + 4, dev_g),
            remote(buf.at[unit(G2)], buf.at[unit(D2)], base + 5, dev_x),
        ]
        return first, second

    cp_code.wait()

    def decode(t, carry):
        r = pl.ds(pl.multiple_of(t * 32, 32), 32)
        to = pl.ds(pl.multiple_of(M1 * UNIT + t * 32, 32), 32)
        sc = scales[r, :]
        scale = jnp.where(sc == -9, 2.0**-18, jnp.where(sc == -8, 2.0**-17, 2.0**-16)).astype(F32)
        for j in range(D // 128):
            code = code_v[r, j * 128 : (j + 1) * 128]
            exp = (code >> 3) & 15
            man = code & 7
            mag = jnp.where(exp == 0, man, (man + 8) << jnp.maximum(exp - 1, 0))
            val = jnp.where(code >= 128, -mag, mag).astype(F32) * scale[:, j : j + 1]
            rin[to, j * 128 : (j + 1) * 128] = val.astype(BF16)
        return carry

    lax.fori_loop(0, 8, decode, 0)
    in_1, in_2 = row_hops(rin, IN_HOP)
    for c in in_1:
        c.start()

    def head(c, carry):
        tok_copy(c).wait()
        go_copy(c).wait()
        for k in range(4):
            i = c * 4 + k
            logits = dot(par_t[...], tok[i], 1, 1)
            e_m = jnp.exp(logits - jnp.max(logits, axis=1, keepdims=True))
            disp[i] = e_m / jnp.sum(e_m, axis=1, keepdims=True)
            e_s = jnp.exp(logits - jnp.max(logits, axis=0, keepdims=True))
            comb_i = e_s / jnp.sum(e_s, axis=0, keepdims=True)
            comb[i] = comb_i
            put(fbuf, pl.ds(pl.multiple_of(i * S, S), S), dot(comb_i.astype(BF16), go[i], 1, 0))
        return carry

    lax.fori_loop(0, 4, head, 0)
    for s in range(S):
        sg_send[s] = every_16th(fbuf, s)
    mine_16 = pl.ds(pl.multiple_of(e * IMG, IMG), IMG)
    at_me = pl.ds(pl.multiple_of(M1 * UNIT + e * IMG, IMG), IMG)
    for dev in others_e:
        remote(sg_send.at[dev[1]], rgr.at[at_me], A2A_G, dev).start()
    rgr[at_me, :] = sg_send[e]

    def wait_15(buf, i):
        both = remote(buf.at[pl.ds(0, 15 * IMG)], buf.at[pl.ds(0, 15 * IMG)], i, dev_x)
        both.wait()

    for c in in_1:
        c.wait_recv()
    for c in in_2:
        c.start()

    def pre(k, lo):
        a, sl = gelu_both(dot(rin[pl.ds(lo, 512), :], win[k], 1, 0))
        hid[k, pl.ds(lo, 512), :] = a.astype(BF16)
        slope[k, pl.ds(lo, 512), :] = sl.astype(BF16)

    cp_win.wait()
    cp_wout.wait()
    pre(0, 512)
    wait_15(rgr, A2A_G)
    gr_1, gr_2 = row_hops(rgr, GR_HOP)
    for c in gr_1:
        c.start()
    for c in in_2:
        c.wait_recv()
    pre(0, 0)
    c_win.wait()
    c_wout.start()
    pre(1, 512)
    for c in gr_1:
        c.wait_recv()
    for c in gr_2:
        c.start()
    pre(1, 0)

    def pre_grad(k, lo):
        hg = dot(rgr[pl.ds(lo, 512), :], wout[k], 1, 1)
        pg[k, pl.ds(lo, 512), :] = (hg * slope[k, pl.ds(lo, 512), :].astype(F32)).astype(BF16)

    pre_grad(0, 512)
    for c in gr_2:
        c.wait_recv()
    pre_grad(0, 0)

    def gwo_dot(k, c):
        return dot(hid[k, :, pl.ds(pl.multiple_of(c * 128, 128), 128)], rgr[...], 0, 0)

    def gwi_dot(k, c):
        return dot(rin[:, pl.ds(pl.multiple_of(c * 256, 256), 256)], pg[k], 0, 0)

    def gwo_copy(c):
        return remote(gwo_s.at[c], gwo_r.at[c], GWO + c, dev_p)

    def gwi_copy(c):
        return remote(gwi_s.at[c], gwi_r.at[c], GWI + c, dev_p)

    def send_gwo(c, carry):
        gwo_s[c] = gwo_dot(1, c).astype(BF16)
        gwo_copy(c).start()
        return carry

    lax.fori_loop(0, 5, send_gwo, 0)

    def part(act, w, cw, r):
        return dot(act[0, r, :], w[0], 1, cw) + dot(act[1, r, :], w[1], 1, cw)

    def rs_hops(ps, rs, h2, base):
        first = [
            remote(ps.at[unit(0, 2)], rs.at[unit(0, 2)], base, dev_x),
            remote(ps.at[unit(2, 2)], rs.at[unit(2, 2)], base + 1, dev_g),
        ]
        second = [
            remote(h2.at[unit(0)], rs.at[unit(4)], base + 2, dev_g),
            remote(h2.at[unit(1)], rs.at[unit(5)], base + 3, dev_x),
        ]
        return first, second

    c_wout.wait()
    out_1, out_2 = rs_hops(ps_o, rs_o, h2_o, OUT_RS)
    ig_1, ig_2 = rs_hops(ps_i, rs_i, h2_i, IG_RS)
    for t in range(2):
        ps_o[unit(2 * t, 2), :] = part(hid, wout, 0, unit(2 * t, 2)).astype(BF16)
        out_1[t].start()
    pre_grad(1, 0)
    for t in range(2):
        ps_i[unit(2 * t, 2), :] = part(pg, win, 1, unit(2 * t, 2)).astype(BF16)
        ig_1[t].start()
    for t in range(2):
        kp_o[unit(2 * t, 2), :] = part(hid, wout, 0, unit(4 + 2 * t, 2))
    pre_grad(1, 512)
    for t in range(2):
        kp_i[unit(2 * t, 2), :] = part(pg, win, 1, unit(4 + 2 * t, 2))

    def second_hop(first, second, kp, rs, h2):
        first[0].wait_recv()
        h2[unit(0), :] = (kp[unit(2), :] + rs[unit(1), :].astype(F32)).astype(BF16)
        second[0].start()
        first[1].wait_recv()
        h2[unit(1), :] = (kp[unit(3), :] + rs[unit(3), :].astype(F32)).astype(BF16)
        second[1].start()

    def finish_rows(second, kp, rs, fin, back, i):
        second[0].wait_recv()
        fin[unit(0), :] = (
            kp[unit(0), :] + rs[unit(0), :].astype(F32) + rs[unit(4), :].astype(F32)
        ).astype(BF16)
        second[1].wait_recv()
        fin[unit(1), :] = (
            kp[unit(1), :] + rs[unit(2), :].astype(F32) + rs[unit(5), :].astype(F32)
        ).astype(BF16)
        for dev in others_e:
            src = pl.ds(pl.multiple_of(dev[1] * IMG, IMG), IMG)
            remote(fin.at[src], back.at[mine_16], i, dev).start()
        back[mine_16, :] = fin[mine_16, :]

    second_hop(out_1, out_2, kp_o, rs_o, h2_o)

    def send_gwi(c, carry):
        gwi_s[c] = gwi_dot(1, c).astype(BF16)
        gwi_copy(c).start()
        return carry

    lax.fori_loop(0, 5, send_gwi, 0)
    second_hop(ig_1, ig_2, kp_i, rs_i, h2_i)
    finish_rows(out_2, kp_o, rs_o, fin_o, back_o, A2A_O)
    finish_rows(ig_2, kp_i, rs_i, fin_i, back_i, A2A_I)

    wait_15(back_o, A2A_O)
    put(fbuf, slice(None), back_o[...].astype(F32))

    def tail_comb(c, carry):
        for k in range(4):
            i = c * 4 + k
            cg = dot(every_16th(fbuf, i), go[i], 1, 1)
            cm = comb[i]
            comb[i] = cm * (cg - jnp.sum(cm * cg, axis=0, keepdims=True))
        return carry

    lax.fori_loop(0, 4, tail_comb, 0)
    wait_15(back_i, A2A_I)
    put(gbuf, slice(None), back_i[...].astype(F32))
    gp_acc[...] = jnp.zeros_like(gp_acc)

    def gt_copy(c):
        return here(tok.at[pl.ds(c * 4, 4)], gt_out.at[pl.ds(c * 4, 4)], L_GT + c)

    def tail(c, carry):
        for k in range(4):
            i = c * 4 + k
            bg = every_16th(gbuf, i)
            dg = dot(bg, tok[i], 1, 1)
            dp = disp[i]
            lg = (comb[i] + dp * (dg - jnp.sum(dp * dg, axis=1, keepdims=True))).astype(BF16)
            gp_acc[...] += dot(lg, tok[i], 1, 0)
            left = jnp.concatenate([dp.astype(BF16), lg], axis=0)
            right = jnp.concatenate([bg, par_t[...]], axis=0)
            tok[i] = dot(left, right, 0, 0).astype(BF16)
        gt_copy(c).start()
        return carry

    lax.fori_loop(0, 4, tail, 0)

    for s in range(S):
        gp_s[s] = gp_acc[s : s + 1, :]
    for dev in others_e:
        remote(gp_s.at[dev[1]], gp_r1.at[e], GP_A, dev).start()
    gp_r1[e] = gp_s[e]

    def finish_gwo(c, carry):
        own = gwo_dot(0, c)
        gwo_copy(c).wait()
        gwo_r[c] = (own + gwo_r[c].astype(F32)).astype(BF16)
        here(gwo_r.at[c], gwo_out.at[0, pl.ds(pl.multiple_of(c * 128, 128), 128)], L_GWO + c).start()
        return carry

    lax.fori_loop(0, 3, finish_gwo, 0)
    wait_many = remote(gp_s.at[pl.ds(0, NE - 1)], gp_r1.at[pl.ds(0, NE - 1)], GP_A, dev_x)
    wait_many.wait()
    total = gp_r1[0]
    for k in range(1, NE):
        total = total + gp_r1[k]
    gp_m[0] = total
    gp_r2[d] = total
    for dev in others_d:
        remote(gp_m.at[0], gp_r2.at[d], GP_B, dev).start()
    lax.fori_loop(3, 5, finish_gwo, 0)
    wait_many = remote(gp_r2.at[pl.ds(0, ND - 1)], gp_r2.at[pl.ds(0, ND - 1)], GP_B, dev_x)
    wait_many.wait()
    total = gp_r2[0]
    for k in range(1, ND):
        total = total + gp_r2[k]
    gp_m[1] = total
    gp_f[e] = total
    for dev in others_e:
        remote(gp_m.at[1], gp_f.at[e], GP_C, dev).start()

    def finish_gwi(c, carry):
        own = gwi_dot(0, c)
        gwi_copy(c).wait()
        gwi_r[c] = (own + gwi_r[c].astype(F32)).astype(BF16)
        here(gwi_r.at[c], gwi_out.at[0, pl.ds(pl.multiple_of(c * 256, 256), 256)], L_GWI + c).start()
        return carry

    lax.fori_loop(0, 5, finish_gwi, 0)
    wait_many = remote(gp_f.at[pl.ds(0, NE - 1)], gp_f.at[pl.ds(0, NE - 1)], GP_C, dev_x)
    wait_many.wait()
    cp_gp = here(gp_f, gp_out, L_GP)
    cp_gp.start()

    for c in in_1 + in_2 + gr_1 + gr_2 + out_1 + out_2 + ig_1 + ig_2:
        c.wait_send()
    for c in range(4):
        gt_copy(c).wait()
    for c in range(5):
        here(gwo_r.at[c], gwo_out.at[0, pl.ds(c * 128, 128)], L_GWO + c).wait()
        here(gwi_r.at[c], gwi_out.at[0, pl.ds(c * 256, 256)], L_GWI + c).wait()
    cp_gp.wait()


def layer(codes, scales, tokens, gout, par_t, w_in, w_out):
    any_space = pl.BlockSpec(memory_space=pl.ANY)
    vmem_space = pl.BlockSpec(memory_space=pltpu.VMEM)

    def buf(*shape, dtype=BF16):
        return pltpu.VMEM(shape, dtype)

    scratch = [
        buf(256, D, dtype=jnp.int32), buf(IMG, PAT, D), buf(IMG, PAT, D), buf(2, D, FU), buf(2, FU, D),
        buf(ROWS, D), buf(ROWS, D), buf(2, ROWS, FU), buf(2, ROWS, FU), buf(2, ROWS, FU),
        buf(IMG, S, PAT, dtype=F32), buf(IMG, S, PAT, dtype=F32), buf(D // 128, 256, 128, dtype=F32), buf(D // 128, 256, 128, dtype=F32),
        buf(S, IMG, D), buf(256, D), buf(256, D),
        buf(512, D), buf(512, D), buf(512, D, dtype=F32), buf(512, D, dtype=F32),
        buf(768, D), buf(768, D), buf(256, D), buf(256, D), buf(256, D), buf(256, D),
        buf(5, 128, D), buf(5, 256, FU), buf(5, 128, D), buf(5, 256, FU),
        buf(S, D, dtype=F32), buf(S, 1, D, dtype=F32), buf(S, 1, D, dtype=F32), buf(2, 1, D, dtype=F32),
        buf(ND, 1, D, dtype=F32), buf(S, 1, D, dtype=F32),
        pltpu.SemaphoreType.DMA((N_SEM,)), pltpu.SemaphoreType.DMA((N_SEM,)), pltpu.SemaphoreType.DMA((N_LOC,)),
    ]
    return pl.pallas_call(
        kernel,
        out_shape=(
            jax.ShapeDtypeStruct((IMG, PAT, D), BF16),
            jax.ShapeDtypeStruct((S, 1, D), F32),
            jax.ShapeDtypeStruct((1, D, FU), BF16),
            jax.ShapeDtypeStruct((1, FU, D), BF16),
        ),
        in_specs=[any_space, vmem_space, any_space, any_space, vmem_space, any_space, any_space],
        out_specs=(any_space,) * 4,
        scratch_shapes=scratch,
        compiler_params=pltpu.CompilerParams(
            collective_id=0, has_side_effects=True, vmem_limit_bytes=63 * 2**20
        ),
        cost_estimate=pl.CostEstimate(flops=21_000_000_000, bytes_accessed=40_000_000, transcendentals=2_000_000),
    )(codes, scales, tokens, gout, par_t, w_in, w_out)


def local(tokens, slot_params, grad_out, slot_codes, scale_exps, w_in, w_out):
    grad_tokens, grad_params, grad_w_in, grad_w_out = layer(
        slot_codes[:, 0], scale_exps[:, 0], tokens, grad_out, slot_params.T, w_in, w_out
    )
    return (grad_tokens, grad_params[:, 0].T, grad_w_in, grad_w_out)


def solution(mesh):
    in_specs = (
        P(("dp", "expert"), None, None),
        P(),
        P(("dp", "expert"), None, None),
        P("dp", "expert", None),
        P("dp", "expert", None),
        P("expert", None, "dp"),
        P("expert", "dp", None),
    )
    out_specs = (
        P(("dp", "expert"), None, None),
        P(),
        P("expert", None, "dp"),
        P("expert", "dp", None),
    )
    return jax.shard_map(local, mesh=mesh, in_specs=in_specs, out_specs=out_specs, check_vma=False)
```

time: 657 us -> 167 us (0.25)
  waiting for transfers between devices: 478 us -> 0 us
  Pallas kernels: 0 us -> 152 us
  matrix products: 103 us -> 0 us
  blocking collectives: 24.6 us -> 0 us
  starting transfers between devices: 15.2 us -> 0 us
  between operations: 14.1 us -> 0.64 us
  other arithmetic: 8.5 us -> 0 us
    all_gather x4 -> x0, waiting for transfers between devices: 347 us -> none  [the longest x1 126 us: local(): lax.all_gather(w_out, 'dp', axis=1, tiled=True)]
    pallas_call x0 -> x1, Pallas kernels: none -> 152 us  [layer(): pl.pallas_call(kernel, out_shape=(jax.ShapeDtypeStruct((IMG, PAT, D), BF1...]
    psum x1 -> x0, waiting for transfers between devices: 130 us -> none  [local(): grad_params = lax.psum(local_params, ('dp', 'expert'))]
    dot_general x13 -> x0, matrix products: 103 us -> none  [the longest x1 16.9 us: local(): jnp.einsum('gsd,gsf->sdf', all_in, shard_pgrad, preferred_element_type=f_...]
    all_to_all x1 -> x0, blocking collectives: 24.6 us -> none  [local(): lax.all_to_all(slot_grad, 'expert', split_axis=1, concat_axis=0, tiled=True)]
    all_to_all x2 -> x0, starting transfers between devices: 14.4 us -> none  [the longest x1 7.23 us: local(): lax.all_to_all(slot_out, 'expert', split_axis=0, concat_axis=1, tiled=True)]
    unnamed x21 -> x10, local copies, waits for them, and re-layouts: 7.46 us -> 14.1 us
  transfers between devices with their start and end apart: 7 -> 0, of which waited for: 5 -> 0; matrix products, arithmetic and copies ran while one was open for 12% -> 0% of each run, Pallas kernels for 0% -> 0%
where the time goes in v1:
time: 167 us; the launch traced here: 166 us
  Pallas kernels  152 us (91%)
  local copies, waits for them, and re-layouts  14.1 us (8%)
    pallas_call x1, Pallas kernels, layer(): pl.pallas_call(kernel, out_shape=(jax.ShapeDtypeStruct((IMG, PAT, D), BF1...  152 us
    unnamed x10, local copies, waits for them, and re-layouts  14.1 us

profile of v1, /device:TPU:1, one launch (start us, length us, event | category | flops | bytes accessed | tf_op | source)
XLA Modules:
  0.0 166.4 jit_solution(6190825873653044006)
XLA Ops:
  0.6 1.5 copy.11
  2.1 2.5 %copy.16 = s32[256,1,1280]{2,0,1:T(8,128)} copy(s32[256,1,1280]{2,1,0:T(1,128)} %param.10) | data formatting | bytes 2621440
  4.6 151.7 %shard_map.102 = (bf16[16,128,1280]{2,1,0:T(8,128)(2,1)}, f32[16,1,1280]{2,1,0:T(1,128)}, bf16[1,1280,640]{2,1,0:T(8,128)(2,1)}, bf16[1,640,1280]{2,1,0:T(8,128)(2,1)}) custom-call(s32[256,1280]{1,0:T(8,128)} %bitcast.10, s32[256,10]{1,0:T(8,128)} %bitcast.11, bf16[16,128,1280]{2,1,0:T(8,128)(2,1)} %tokens.1, bf16[16,128,1280]{2,1,0:T(8,128)(2,1)} %gout.1, ...), custom_call_target="tpu_custom_call" | custom-call | flops 20999999488 | bytes 40000000 | tf_op jit(solution)/shard_map/pallas_call | solution.py:402
  156.2 1.5 copy.17
  157.8 0.0 copy-start.1
  157.8 5.4 %copy.21 = bf16[16,128,1280]{2,1,0:T(8,128)(2,1)} copy(bf16[16,128,1280]{2,1,0:T(8,128)(2,1)} %get-tuple-element.16) | data formatting | bytes 10485760
  163.2 0.0 copy-done.1
  163.2 0.0 copy-start
  163.2 1.2 copy.22
  164.4 0.9 copy-done
  165.2 1.2 copy.23
Async XLA Ops:
  157.8 5.5 %copy-start.1 = (bf16[1,1280,640]{2,1,0:T(8,128)(2,1)S(1)}, bf16[1,1280,640]{2,1,0:T(8,128)(2,1)}, u32[]{:S(2)}) copy-start(bf16[1,1280,640]{2,1,0:T(8,128)(2,1)} %get-tuple-element.18) | copy-start | bytes 4915204
  163.2 2.0 %copy-start = (bf16[1,640,1280]{2,1,0:T(8,128)(2,1)S(1)}, bf16[1,640,1280]{2,1,0:T(8,128)(2,1)}, u32[]{:S(2)}) copy-start(bf16[1,640,1280]{2,1,0:T(8,128)(2,1)} %get-tuple-element.19) | copy-start | bytes 4915204

commit v2 on v1

v2 whole, which is shorter than its diff:
```python
import jax
import jax.numpy as jnp
from jax import lax
from jax.experimental import pallas as pl
from jax.experimental.pallas import tpu as pltpu
from jax.sharding import PartitionSpec as P

F32 = jnp.float32
BF16 = jnp.bfloat16
MESH = pl.DeviceIdType.MESH
gelu_coef = 0.7978845608028654

D, FU = 1280, 640
IMG, PAT, S = 16, 128, 16
ROWS = 1024
ND, NE = 8, 16

N1, N2 = 64, 192
X1, D1, G2, D2 = (0, N1), (64, N1), (128, N2), (320, N2)
M1, M2, G1, X2 = (512, N1), (576, N2), (768, N1), (832, N2)
ME = 512
KEEP = 512

W_IN, W_OUT = 0, 1
IN_HOP, GR_HOP, OUT_RS, IG_RS = 2, 9, 16, 20
GWO, GWI = 24, 29
A2A_G, A2A_O, A2A_I = 34, 35, 36
GP_A, GP_B, GP_C = 37, 38, 39
N_SEM = 40
L_CODE, L_WIN, L_WOUT, L_TOK, L_GO, L_LEFT, L_BG, L_SC, L_GWO, L_GWI, L_GP = 0, 1, 2, 3, 7, 11, 12, 13, 15, 20, 25
N_LOC = 26


def dot(a, b, ca, cb):
    return lax.dot_general(a, b, (((ca,), (cb,)), ((), ())), preferred_element_type=F32)


def gelu_both(x):
    x2 = x * x
    t = jnp.tanh(gelu_coef * (x + 0.044715 * x * x2))
    h = 0.5 * (1.0 + t)
    return x * h, h + 0.5 * x * (1.0 - t * t) * (gelu_coef + (gelu_coef * 3.0 * 0.044715) * x2)


def unit(u, skip=0, n=None):
    return pl.ds(u[0] + skip, n or u[1] - skip)


def put(ref, rows, value):
    for j in range(D // 128):
        ref[j, rows, :] = value[:, j * 128 : (j + 1) * 128]


def every_16th(ref, start):
    return jnp.concatenate([ref[j, pl.ds(start, 16, stride=16), :].astype(BF16) for j in range(D // 128)], axis=1)


def kernel(
    codes, scales, tokens, gout, par_t, w_in, w_out,
    left_out, bg_out, gp_out, gwi_out, gwo_out,
    code_v, sc_v, tok, go, win, wout, rin, rgr, hid, slope, pg,
    comb, disp, fbuf, gbuf, sg_send, back_o, back_i,
    ps_o, ps_i, kp_o, kp_i, rs_o, rs_i, h2_o, h2_i, fin_o, fin_i,
    gwo_s, gwi_s, gwo_r, gwi_r, gp_acc, gp_s, gp_r1, gp_m, gp_r2, gp_f, left, bgi, lg_all, gwi_own,
    s_sem, r_sem, l_sem,
):
    d, e = lax.axis_index("dp"), lax.axis_index("expert")
    xl, z, core = d // 4, lax.rem(d, 4), lax.rem(e, 2)
    z_near = z + 1 - 2 * lax.rem(z, 2)
    z_far = 3 - z
    z_pair = z_near * (1 - core) + z_far * core
    z_group = z_far * (1 - core) + z_near * core
    dev_x = ((1 - xl) * 4 + z, e)
    dev_p = (xl * 4 + z_pair, e)
    dev_g = (xl * 4 + z_group, e)
    others_e = [(d, lax.rem(e + k, NE)) for k in range(1, NE)]
    others_d = [(lax.rem(d + k, ND), e) for k in range(1, ND)]

    def remote(src, dst, i, dev):
        return pltpu.make_async_remote_copy(
            src_ref=src, dst_ref=dst, send_sem=s_sem.at[i], recv_sem=r_sem.at[i], device_id=dev, device_id_type=MESH
        )

    def here(src, dst, i):
        return pltpu.make_async_copy(src, dst, l_sem.at[i])

    cp_code = here(codes.at[:, 0], code_v, L_CODE)
    cp_win = here(w_in.at[0], win.at[0], L_WIN)
    cp_wout = here(w_out.at[0], wout.at[0], L_WOUT)
    cp_sc = here(scales.at[:, 0], sc_v, L_SC)
    cp_code.start()
    cp_sc.start()

    def four(c):
        return pl.ds(pl.multiple_of(c * 4 * PAT, 4 * PAT), 4 * PAT)

    def image(i):
        return pl.ds(pl.multiple_of(i * PAT, PAT), PAT)

    def tok_copy(c):
        return here(tokens.at[four(c)], tok.at[four(c)], L_TOK + c)

    def go_copy(c):
        return here(gout.at[four(c)], go.at[four(c)], L_GO + c)

    barrier = pltpu.get_barrier_semaphore()
    for dev in others_e + others_d:
        pl.semaphore_signal(barrier, inc=1, device_id=dev, device_id_type=MESH)
    pl.semaphore_wait(barrier, NE + ND - 2)

    c_win = remote(w_in.at[0], win.at[1], W_IN, dev_p)
    c_wout = remote(w_out.at[0], wout.at[1], W_OUT, dev_p)
    c_win.start()

    def row_hops(buf, base):
        first = [
            remote(buf.at[unit(M1)], buf.at[unit(X1)], base, dev_x),
            remote(buf.at[unit(M2)], buf.at[unit(G2)], base + 1, dev_g),
            remote(buf.at[unit(M2)], buf.at[unit(X2)], base + 2, dev_x),
            remote(buf.at[unit(M1)], buf.at[unit(G1)], base + 3, dev_g),
        ]
        second = [
            remote(buf.at[unit(X1)], buf.at[unit(D1)], base + 4, dev_g),
            remote(buf.at[unit(X2, 0, 64)], buf.at[unit(D2, 0, 64)], base + 5, dev_g),
            remote(buf.at[unit(G2, 64)], buf.at[unit(D2, 64)], base + 6, dev_x),
        ]
        return first, second

    cp_code.wait()
    cp_sc.wait()

    sc = sc_v[...]
    fbuf[0, :, : D // 128] = jnp.where(sc == -9, 2.0**-18, jnp.where(sc == -8, 2.0**-17, 2.0**-16)).astype(F32).T

    def decode(t, carry):
        r = pl.ds(pl.multiple_of(t * 32, 32), 32)
        to = pl.ds(pl.multiple_of(ME + t * 32, 32), 32)
        scale = fbuf[0, r, : D // 128]
        for j in range(D // 128):
            code = code_v[r, j * 128 : (j + 1) * 128]
            exp = (code >> 3) & 15
            man = code & 7
            mag = jnp.where(exp == 0, man, (man + 8) << jnp.maximum(exp - 1, 0))
            val = jnp.where(code >= 128, -mag, mag).astype(F32) * scale[:, j : j + 1]
            rin[to, j * 128 : (j + 1) * 128] = val.astype(BF16)
        return carry

    lax.fori_loop(0, 8, decode, 0)
    in_1, in_2 = row_hops(rin, IN_HOP)
    for c in in_1:
        c.start()
    for c in range(4):
        tok_copy(c).start()
        go_copy(c).start()
    cp_win.start()
    cp_wout.start()

    def head(c, carry):
        tok_copy(c).wait()
        go_copy(c).wait()
        for k in range(4):
            i = c * 4 + k
            logits = dot(par_t[...], tok[image(i), :], 1, 1)
            e_m = jnp.exp(logits - jnp.max(logits, axis=1, keepdims=True))
            disp[i] = e_m / jnp.sum(e_m, axis=1, keepdims=True)
            e_s = jnp.exp(logits - jnp.max(logits, axis=0, keepdims=True))
            comb_i = e_s / jnp.sum(e_s, axis=0, keepdims=True)
            comb[i] = comb_i
            put(fbuf, pl.ds(pl.multiple_of(i * S, S), S), dot(comb_i.astype(BF16), go[image(i), :], 1, 0))
        return carry

    lax.fori_loop(0, 4, head, 0)
    for s in range(S):
        sg_send[s] = every_16th(fbuf, s)
    mine_16 = pl.ds(pl.multiple_of(e * IMG, IMG), IMG)
    at_me = pl.ds(pl.multiple_of(ME + e * IMG, IMG), IMG)
    for dev in others_e:
        remote(sg_send.at[dev[1]], rgr.at[at_me], A2A_G, dev).start()
    rgr[at_me, :] = sg_send[e]

    def wait_15(buf, i):
        both = remote(buf.at[pl.ds(0, 15 * IMG)], buf.at[pl.ds(0, 15 * IMG)], i, dev_x)
        both.wait()

    for c in in_1:
        c.wait_recv()
    for c in in_2:
        c.start()

    def pre(k, lo):
        a, sl = gelu_both(dot(rin[pl.ds(lo, 512), :], win[k], 1, 0))
        hid[k, pl.ds(lo, 512), :] = a.astype(BF16)
        slope[k, pl.ds(lo, 512), :] = sl.astype(BF16)

    cp_win.wait()
    cp_wout.wait()
    pre(0, 512)
    wait_15(rgr, A2A_G)
    gr_1, gr_2 = row_hops(rgr, GR_HOP)
    for c in gr_1:
        c.start()
    c_win.wait()
    c_wout.start()
    for c in in_2:
        c.wait_recv()
    pre(0, 0)
    pre(1, 512)
    for c in gr_1:
        c.wait_recv()
    for c in gr_2:
        c.start()
    pre(1, 0)

    def pre_grad(k, lo):
        hg = dot(rgr[pl.ds(lo, 512), :], wout[k], 1, 1)
        pg[k, pl.ds(lo, 512), :] = (hg * slope[k, pl.ds(lo, 512), :].astype(F32)).astype(BF16)

    pre_grad(0, 512)
    for c in gr_2:
        c.wait_recv()
    pre_grad(0, 0)

    def gwo_dot(k, c):
        return dot(hid[k, :, pl.ds(pl.multiple_of(c * 128, 128), 128)], rgr[...], 0, 0)

    def gwi_dot(k, c):
        return dot(rin[:, pl.ds(pl.multiple_of(c * 256, 256), 256)], pg[k], 0, 0)

    def gwo_copy(c):
        return remote(gwo_s.at[c], gwo_r.at[c], GWO + c, dev_p)

    def gwi_copy(c):
        return remote(gwi_s.at[c], gwi_r.at[c], GWI + c, dev_p)

    def fill_gwo(c, carry):
        gwo_s[c] = gwo_dot(1, c).astype(BF16)
        return carry

    lax.fori_loop(0, 5, fill_gwo, 0)

    def part(act, w, cw, r):
        return dot(act[0, r, :], w[0], 1, cw) + dot(act[1, r, :], w[1], 1, cw)

    def rs_hops(ps, rs, h2, base):
        first = [
            remote(ps.at[pl.ds(0, 2 * N1)], rs.at[pl.ds(0, 2 * N1)], base, dev_x),
            remote(ps.at[pl.ds(2 * N1, 2 * N2)], rs.at[pl.ds(2 * N1, 2 * N2)], base + 1, dev_g),
        ]
        second = [
            remote(h2.at[pl.ds(0, N1)], rs.at[pl.ds(512, N1)], base + 2, dev_g),
            remote(h2.at[pl.ds(N1, N2)], rs.at[pl.ds(512 + N1, N2)], base + 3, dev_x),
        ]
        return first, second

    def send_parts(act, w, cw, ps, first):
        for t in (1, 0):
            r = (pl.ds(0, 2 * N1), pl.ds(2 * N1, 2 * N2))[t]
            ps[r, :] = part(act, w, cw, r).astype(BF16)
            first[t].start()

    def keep_parts(act, w, cw, kp):
        for t in range(2):
            kp[pl.ds(t * 256, 256), :] = part(act, w, cw, pl.ds(KEEP + t * 256, 256))

    c_wout.wait()
    gwo_copy(0).start()
    out_1, out_2 = rs_hops(ps_o, rs_o, h2_o, OUT_RS)
    ig_1, ig_2 = rs_hops(ps_i, rs_i, h2_i, IG_RS)
    send_parts(hid, wout, 0, ps_o, out_1)
    pre_grad(1, 0)
    send_parts(pg, win, 1, ps_i, ig_1)
    keep_parts(hid, wout, 0, kp_o)
    pre_grad(1, 512)
    keep_parts(pg, win, 1, kp_i)

    def second_hop(first, second, kp, rs, h2):
        first[1].wait_recv()
        got = rs[pl.ds(2 * N1 + N2, N2), :].astype(F32)
        h2[pl.ds(N1, N2), :] = (kp[pl.ds(256 + N1, N2), :] + got).astype(BF16)
        second[1].start()
        first[0].wait_recv()
        got = rs[pl.ds(N1, N1), :].astype(F32)
        h2[pl.ds(0, N1), :] = (kp[pl.ds(256, N1), :] + got).astype(BF16)
        second[0].start()

    def finish_rows(second, kp, rs, fin, back, i):
        second[0].wait_recv()
        a, b, c = pl.ds(0, N1), pl.ds(0, N1), pl.ds(512, N1)
        fin[a, :] = (kp[a, :] + rs[b, :].astype(F32) + rs[c, :].astype(F32)).astype(BF16)
        second[1].wait_recv()
        a, b, c = pl.ds(N1, N2), pl.ds(2 * N1, N2), pl.ds(512 + N1, N2)
        fin[a, :] = (kp[a, :] + rs[b, :].astype(F32) + rs[c, :].astype(F32)).astype(BF16)
        for dev in others_e:
            src = pl.ds(pl.multiple_of(dev[1] * IMG, IMG), IMG)
            remote(fin.at[src], back.at[mine_16], i, dev).start()
        back[mine_16, :] = fin[mine_16, :]

    second_hop(out_1, out_2, kp_o, rs_o, h2_o)
    gwo_copy(1).start()

    def fill_gwi(c, carry):
        gwi_s[c] = gwi_dot(1, c).astype(BF16)
        return carry

    lax.fori_loop(0, 5, fill_gwi, 0)
    second_hop(ig_1, ig_2, kp_i, rs_i, h2_i)
    for c in range(2, 5):
        gwo_copy(c).start()
    for c in range(5):
        gwi_copy(c).start()
    finish_rows(out_2, kp_o, rs_o, fin_o, back_o, A2A_O)

    def fill_own(c, carry):
        gwi_own[c] = gwi_dot(0, c)
        return carry

    lax.fori_loop(0, 5, fill_own, 0)
    finish_rows(ig_2, kp_i, rs_i, fin_i, back_i, A2A_I)

    def finish_gwo(c, carry):
        own = gwo_dot(0, c)
        gwo_copy(c).wait()
        gwo_r[c] = (own + gwo_r[c].astype(F32)).astype(BF16)
        here(gwo_r.at[c], gwo_out.at[pl.ds(pl.multiple_of(c * 128, 128), 128)], L_GWO + c).start()
        return carry

    def finish_gwi(c, carry):
        gwi_copy(c).wait()
        gwi_r[c] = (gwi_own[c] + gwi_r[c].astype(F32)).astype(BF16)
        here(gwi_r.at[c], gwi_out.at[pl.ds(pl.multiple_of(c * 256, 256), 256)], L_GWI + c).start()
        return carry

    wait_15(back_o, A2A_O)
    put(fbuf, slice(None), back_o[...].astype(F32))

    def tail_comb(c, carry):
        for k in range(4):
            i = c * 4 + k
            cg = dot(every_16th(fbuf, i), go[image(i), :], 1, 1)
            cm = comb[i]
            comb[i] = cm * (cg - jnp.sum(cm * cg, axis=0, keepdims=True))
        return carry

    lax.fori_loop(0, 4, tail_comb, 0)
    wait_15(back_i, A2A_I)
    put(gbuf, slice(None), back_i[...].astype(F32))

    cp_left = here(left, left_out, L_LEFT)
    cp_bg = here(bgi, bg_out, L_BG)

    def tail(c, carry):
        for k in range(4):
            i = c * 4 + k
            bg = every_16th(gbuf, i)
            dg = dot(bg, tok[image(i), :], 1, 1)
            dp = disp[i]
            lg = (comb[i] + dp * (dg - jnp.sum(dp * dg, axis=1, keepdims=True))).astype(BF16)
            lg_all[:, image(i)] = lg
            left[i, :S] = dp.astype(BF16)
            left[i, S:] = lg
            bgi[i] = bg
        return carry

    lax.fori_loop(0, 4, tail, 0)
    cp_left.start()
    cp_bg.start()

    gp = dot(lg_all[...], tok[...], 1, 0)
    for s in range(S):
        gp_s[s] = gp[s : s + 1, :]
    for dev in others_e:
        remote(gp_s.at[dev[1]], gp_r1.at[e], GP_A, dev).start()
    gp_r1[e] = gp_s[e]

    lax.fori_loop(0, 5, finish_gwo, 0)
    wait_many = remote(gp_s.at[pl.ds(0, NE - 1)], gp_r1.at[pl.ds(0, NE - 1)], GP_A, dev_x)
    wait_many.wait()
    total = gp_r1[0]
    for k in range(1, NE):
        total = total + gp_r1[k]
    gp_m[0] = total
    gp_r2[d] = total
    for dev in others_d:
        remote(gp_m.at[0], gp_r2.at[d], GP_B, dev).start()
    lax.fori_loop(0, 2, finish_gwi, 0)
    wait_many = remote(gp_r2.at[pl.ds(0, ND - 1)], gp_r2.at[pl.ds(0, ND - 1)], GP_B, dev_x)
    wait_many.wait()
    total = gp_r2[0]
    for k in range(1, ND):
        total = total + gp_r2[k]
    gp_m[1] = total
    gp_f[e] = total
    for dev in others_e:
        remote(gp_m.at[1], gp_f.at[e], GP_C, dev).start()

    lax.fori_loop(2, 5, finish_gwi, 0)
    wait_many = remote(gp_f.at[pl.ds(0, NE - 1)], gp_f.at[pl.ds(0, NE - 1)], GP_C, dev_x)
    wait_many.wait()
    for s in range(S):
        gp_acc[s : s + 1, :] = gp_f[s]
    cp_gp = here(gp_acc, gp_out, L_GP)
    cp_gp.start()

    for c in in_1 + in_2 + gr_1 + gr_2 + out_1 + out_2 + ig_1 + ig_2:
        c.wait_send()
    cp_left.wait()
    cp_bg.wait()
    for c in range(5):
        here(gwo_r.at[c], gwo_out.at[pl.ds(c * 128, 128)], L_GWO + c).wait()
        here(gwi_r.at[c], gwi_out.at[pl.ds(c * 256, 256)], L_GWI + c).wait()
    cp_gp.wait()


def layer(codes, scales, tokens, gout, par_t, w_in, w_out):
    any_space = pl.BlockSpec(memory_space=pl.ANY)
    vmem_space = pl.BlockSpec(memory_space=pltpu.VMEM)

    def buf(*shape, dtype=BF16):
        return pltpu.VMEM(shape, dtype)

    scratch = [
        buf(256, D, dtype=jnp.int32), buf(D // 128, 256, dtype=jnp.int32), buf(IMG * PAT, D), buf(IMG * PAT, D), buf(2, D, FU), buf(2, FU, D),
        buf(ROWS, D), buf(ROWS, D), buf(2, ROWS, FU), buf(2, ROWS, FU), buf(2, ROWS, FU),
        buf(IMG, S, PAT, dtype=F32), buf(IMG, S, PAT, dtype=F32), buf(D // 128, 256, 128, dtype=F32), buf(D // 128, 256, 128, dtype=F32),
        buf(S, IMG, D), buf(256, D), buf(256, D),
        buf(512, D), buf(512, D), buf(512, D, dtype=F32), buf(512, D, dtype=F32),
        buf(768, D), buf(768, D), buf(256, D), buf(256, D), buf(256, D), buf(256, D),
        buf(5, 128, D), buf(5, 256, FU), buf(5, 128, D), buf(5, 256, FU),
        buf(S, D, dtype=F32), buf(S, 1, D, dtype=F32), buf(S, 1, D, dtype=F32), buf(2, 1, D, dtype=F32),
        buf(ND, 1, D, dtype=F32), buf(S, 1, D, dtype=F32), buf(IMG, 2 * S, PAT), buf(IMG, S, D), buf(S, IMG * PAT),
        buf(5, 256, FU, dtype=F32),
        pltpu.SemaphoreType.DMA((N_SEM,)), pltpu.SemaphoreType.DMA((N_SEM,)), pltpu.SemaphoreType.DMA((N_LOC,)),
    ]
    return pl.pallas_call(
        kernel,
        out_shape=(
            jax.ShapeDtypeStruct((IMG, 2 * S, PAT), BF16),
            jax.ShapeDtypeStruct((IMG, S, D), BF16),
            jax.ShapeDtypeStruct((S, D), F32),
            jax.ShapeDtypeStruct((D, FU), BF16),
            jax.ShapeDtypeStruct((FU, D), BF16),
        ),
        in_specs=[any_space, any_space, any_space, any_space, vmem_space, any_space, any_space],
        out_specs=(any_space,) * 5,
        scratch_shapes=scratch,
        compiler_params=pltpu.CompilerParams(
            collective_id=0, has_side_effects=True, vmem_limit_bytes=63 * 2**20
        ),
        cost_estimate=pl.CostEstimate(flops=21_000_000_000, bytes_accessed=40_000_000, transcendentals=2_000_000),
    )(codes, scales, tokens, gout, par_t, w_in, w_out)


def results_kernel(left, bg, par_t, gp, gwi, gwo, gt_o, gp_o, gwi_o, gwo_o):
    for k in range(left.shape[0]):
        right = jnp.concatenate([bg[k], par_t[...]], axis=0)
        gt_o[k] = dot(left[k], right, 0, 0).astype(BF16)
    gp_o[...] = gp[...]
    gwi_o[0] = gwi[...]
    gwo_o[0] = gwo[...]


def results(left, bg, par_t, gp, gwi, gwo):
    n = 2

    def whole(*shape):
        return pl.BlockSpec(shape, lambda i: (0,) * len(shape))

    def parts(*shape):
        return pl.BlockSpec(shape, lambda i: (i,) + (0,) * (len(shape) - 1))

    def rows(*shape):
        return pl.BlockSpec(shape, lambda i: (0, i, 0))

    return pl.pallas_call(
        results_kernel,
        grid=(n,),
        out_shape=(
            jax.ShapeDtypeStruct((IMG, PAT, D), BF16),
            jax.ShapeDtypeStruct((S, D), F32),
            jax.ShapeDtypeStruct((1, D, FU), BF16),
            jax.ShapeDtypeStruct((1, FU, D), BF16),
        ),
        in_specs=[
            parts(IMG // n, 2 * S, PAT), parts(IMG // n, S, D), whole(S, D), whole(S, D),
            parts(D // n, FU), parts(FU // n, D),
        ],
        out_specs=(parts(IMG // n, PAT, D), whole(S, D), rows(1, D // n, FU), rows(1, FU // n, D)),
        compiler_params=pltpu.CompilerParams(vmem_limit_bytes=60 * 2**20),
    )(left, bg, par_t, gp, gwi, gwo)


def local(tokens, slot_params, grad_out, slot_codes, scale_exps, w_in, w_out):
    par_t = slot_params.T
    left, bg, gp, gwi, gwo = layer(slot_codes, scale_exps.transpose(2, 1, 0), tokens.reshape(-1, D), grad_out.reshape(-1, D), par_t, w_in, w_out)
    grad_tokens, grad_params, grad_w_in, grad_w_out = results(left, bg, par_t, gp, gwi, gwo)
    return (grad_tokens, grad_params.T, grad_w_in, grad_w_out)


def solution(mesh):
    in_specs = (
        P(("dp", "expert"), None, None),
        P(),
        P(("dp", "expert"), None, None),
        P("dp", "expert", None),
        P("dp", "expert", None),
        P("expert", None, "dp"),
        P("expert", "dp", None),
    )
    out_specs = (
        P(("dp", "expert"), None, None),
        P(),
        P("expert", None, "dp"),
        P("expert", "dp", None),
    )
    return jax.shard_map(local, mesh=mesh, in_specs=in_specs, out_specs=out_specs, check_vma=False)
```

time: 167 us -> 151 us (0.904)
  local copies, waits for them, and re-layouts: 14.1 us -> 0 us
  Pallas kernels: 152 us -> 150 us
    unnamed x10 -> x0, local copies, waits for them, and re-layouts: 14.1 us -> none
    pallas_call x1 -> x2, Pallas kernels: 152 us -> 150 us  [the longest x1 145 us: layer(): pl.pallas_call(kernel, out_shape=(jax.ShapeDtypeStruct((IMG, 2 * S, PAT),...]
where the time goes in v2:
time: 151 us
  Pallas kernels  150 us (99%)
    pallas_call x1, Pallas kernels, layer(): pl.pallas_call(kernel, out_shape=(jax.ShapeDtypeStruct((IMG, 2 * S, PAT),...  145 us
    pallas_call x1, Pallas kernels, results(): pl.pallas_call(results_kernel, grid=(n,), out_shape=(jax.ShapeDtypeStruct...  5.87 us

profile of v2, /device:TPU:1, one launch (start us, length us, event | category | flops | bytes accessed | tf_op | source)
XLA Modules:
  0.0 151.1 jit_solution(7360649506533769133)
XLA Ops:
  0.6 144.6 %shard_map.102 = (bf16[16,32,128]{2,1,0:T(8,128)(2,1)}, bf16[16,16,1280]{2,1,0:T(8,128)(2,1)}, f32[16,1280]{1,0:T(8,128)}, bf16[1280,640]{1,0:T(8,128)(2,1)}, bf16[640,1280]{1,0:T(8,128)(2,1)}) custom-call(s32[256,1,1280]{2,1,0:T(1,128)} %codes.1, s32[10,1,256]{2,1,0:T(1,128)} %bitcast.10, bf16[2048,1280]{1,0:T(8,128)(2,1)} %bitcast.7, ...), custom_call_target="tpu_custom_call" | custom-call | flops 20999999488 | bytes 40000000 | tf_op jit(solution)/shard_map/pallas_call | solution.py:434
  145.2 5.9 %shard_map.103 = (bf16[16,128,1280]{2,1,0:T(8,128)(2,1)}, f32[16,1280]{1,0:T(8,128)}, bf16[1,1280,640]{2,1,0:T(8,128)(2,1)}, bf16[1,640,1280]{2,1,0:T(8,128)(2,1)}) custom-call(bf16[16,32,128]{2,1,0:T(8,128)(2,1)} %get-tuple-element.13.left, bf16[16,16,1280]{2,1,0:T(8,128)(2,1)} %get-tuple-element.14.bg, bf16[16,1280]{1,0:T(8,128)(2,1)} %bitcast.6, ...), custom_call_target="tpu_custom_call" | custom-call | tf_op jit(solution)/shard_map/pallas_call | solution.py:474

commit v3 on v2

--- a/solution.py
+++ b/solution.py
@@ -20,13 +20,14 @@
 M1, M2, G1, X2 = (512, N1), (576, N2), (768, N1), (832, N2)
 ME = 512
 KEEP = 512
+AWAY = 128
 
 W_IN, W_OUT = 0, 1
-IN_HOP, GR_HOP, OUT_RS, IG_RS = 2, 9, 16, 20
-GWO, GWI = 24, 29
-A2A_G, A2A_O, A2A_I = 34, 35, 36
-GP_A, GP_B, GP_C = 37, 38, 39
-N_SEM = 40
+IN_HOP, GR_HOP, OUT_RS, IG_RS = 2, 11, 18, 22
+GWO, GWI = 26, 31
+A2A_G, A2A_O, A2A_I = 36, 37, 38
+GP_A, GP_B, GP_C = 39, 40, 41
+N_SEM = 42
 L_CODE, L_WIN, L_WOUT, L_TOK, L_GO, L_LEFT, L_BG, L_SC, L_GWO, L_GWI, L_GP = 0, 1, 2, 3, 7, 11, 12, 13, 15, 20, 25
 N_LOC = 26
 
@@ -75,6 +76,18 @@
     dev_g = (xl * 4 + z_group, e)
     others_e = [(d, lax.rem(e + k, NE)) for k in range(1, NE)]
     others_d = [(lax.rem(d + k, ND), e) for k in range(1, ND)]
+    y, xh = e // 4, lax.rem(e // 2, 2)
+    d_x = (1 - xl) * 4 + z
+
+    def expert(j, k, x_hi):
+        return lax.rem(y + j, 4) * 4 + x_hi * 2 + lax.rem(core + k, 2)
+
+    def eighth(a):
+        return (a // 4) * 2 + lax.rem(a, 2)
+
+    turns = [(j, k) for j in range(4) for k in range(2)]
+    home = [(d, expert(j, k, xh)) for j, k in turns[1:]]
+    away = [(d_x, expert(j, k, 1 - xh)) for j, k in turns]
 
     def remote(src, dst, i, dev):
         return pltpu.make_async_remote_copy(
@@ -104,13 +117,31 @@
         return here(gout.at[four(c)], go.at[four(c)], L_GO + c)
 
     barrier = pltpu.get_barrier_semaphore()
-    for dev in others_e + others_d:
+    for dev in others_e + others_d + away:
         pl.semaphore_signal(barrier, inc=1, device_id=dev, device_id_type=MESH)
-    pl.semaphore_wait(barrier, NE + ND - 2)
+    pl.semaphore_wait(barrier, NE + ND - 2 + 8)
 
     c_win = remote(w_in.at[0], win.at[1], W_IN, dev_p)
     c_wout = remote(w_out.at[0], wout.at[1], W_OUT, dev_p)
     c_win.start()
+
+    def second_hops(buf, base, to):
+        return [
+            remote(buf.at[unit(X1)], buf.at[unit(D1)], base, dev_g),
+            remote(buf.at[unit(X2, 0, 64)], buf.at[unit(D2, 0, 64)], base + 1, dev_g),
+            remote(buf.at[unit(to[0], 64)], buf.at[unit(to[1], 64)], base + 2, dev_x),
+        ]
+
+    def in_hops(buf, base):
+        first = [
+            remote(buf.at[unit(M1)], buf.at[unit(X1)], base, dev_x),
+            remote(buf.at[unit(X2, 64)], buf.at[unit(D2, 64)], base + 1, dev_g),
+            remote(buf.at[unit(M2, 0, 64)], buf.at[unit(X2, 0, 64)], base + 2, dev_x),
+            remote(buf.at[unit(M1)], buf.at[unit(G1)], base + 3, dev_g),
+            remote(buf.at[unit(X2, 64)], buf.at[unit(M2, 64)], base + 4, dev_x),
+            remote(buf.at[unit(M2, 0, 64)], buf.at[unit(G2, 0, 64)], base + 5, dev_g),
+        ]
+        return first, second_hops(buf, base + 6, (D2, G2))
 
     def row_hops(buf, base):
         first = [
@@ -119,12 +150,7 @@
             remote(buf.at[unit(M2)], buf.at[unit(X2)], base + 2, dev_x),
             remote(buf.at[unit(M1)], buf.at[unit(G1)], base + 3, dev_g),
         ]
-        second = [
-            remote(buf.at[unit(X1)], buf.at[unit(D1)], base + 4, dev_g),
-            remote(buf.at[unit(X2, 0, 64)], buf.at[unit(D2, 0, 64)], base + 5, dev_g),
-            remote(buf.at[unit(G2, 64)], buf.at[unit(D2, 64)], base + 6, dev_x),
-        ]
-        return first, second
+        return first, second_hops(buf, base + 4, (G2, D2))
 
     cp_code.wait()
     cp_sc.wait()
@@ -134,7 +160,9 @@
 
     def decode(t, carry):
         r = pl.ds(pl.multiple_of(t * 32, 32), 32)
-        to = pl.ds(pl.multiple_of(ME + t * 32, 32), 32)
+        off = lax.rem(t, 2) - xh
+        first = ME + off * off * (X2[0] + AWAY - N1 - ME)
+        to = pl.ds(pl.multiple_of(first + (t // 2) * 32, 32), 32)
         scale = fbuf[0, r, : D // 128]
         for j in range(D // 128):
             code = code_v[r, j * 128 : (j + 1) * 128]
@@ -146,7 +174,7 @@
         return carry
 
     lax.fori_loop(0, 8, decode, 0)
-    in_1, in_2 = row_hops(rin, IN_HOP)
+    in_1, in_2 = in_hops(rin, IN_HOP)
     for c in in_1:
         c.start()
     for c in range(4):
@@ -173,10 +201,13 @@
     for s in range(S):
         sg_send[s] = every_16th(fbuf, s)
     mine_16 = pl.ds(pl.multiple_of(e * IMG, IMG), IMG)
-    at_me = pl.ds(pl.multiple_of(ME + e * IMG, IMG), IMG)
-    for dev in others_e:
-        remote(sg_send.at[dev[1]], rgr.at[at_me], A2A_G, dev).start()
-    rgr[at_me, :] = sg_send[e]
+    at_home = pl.ds(pl.multiple_of(ME + eighth(e) * IMG, IMG), IMG)
+    at_away = pl.ds(pl.multiple_of(ME + AWAY + eighth(e) * IMG, IMG), IMG)
+    for dev in home:
+        remote(sg_send.at[dev[1]], rgr.at[at_home], A2A_G, dev).start()
+    for dev in away:
+        remote(sg_send.at[dev[1]], rgr.at[at_away], A2A_G, dev).start()
+    rgr[at_home, :] = sg_send[e]
 
     def wait_15(buf, i):
         both = remote(buf.at[pl.ds(0, 15 * IMG)], buf.at[pl.ds(0, 15 * IMG)], i, dev_x)
@@ -290,10 +321,13 @@
         second[1].wait_recv()
         a, b, c = pl.ds(N1, N2), pl.ds(2 * N1, N2), pl.ds(512 + N1, N2)
         fin[a, :] = (kp[a, :] + rs[b, :].astype(F32) + rs[c, :].astype(F32)).astype(BF16)
-        for dev in others_e:
-            src = pl.ds(pl.multiple_of(dev[1] * IMG, IMG), IMG)
+        for dev in home:
+            src = pl.ds(pl.multiple_of(eighth(dev[1]) * IMG, IMG), IMG)
             remote(fin.at[src], back.at[mine_16], i, dev).start()
-        back[mine_16, :] = fin[mine_16, :]
+        for dev in away:
+            src = pl.ds(pl.multiple_of(AWAY + eighth(dev[1]) * IMG, IMG), IMG)
+            remote(fin.at[src], back.at[mine_16], i, dev).start()
+        back[mine_16, :] = fin[pl.ds(pl.multiple_of(eighth(e) * IMG, IMG), IMG), :]
 
     second_hop(out_1, out_2, kp_o, rs_o, h2_o)
     gwo_copy(1).start()

time: 151 us -> 146 us (0.967)
  Pallas kernels: 150 us -> 145 us
    pallas_call x1, Pallas kernels: 145 us -> 139 us  [layer(): pl.pallas_call(kernel, out_shape=(jax.ShapeDtypeStruct((IMG, 2 * S, PAT),...]
where the time goes in v3:
time: 146 us; the launch traced here: 145 us
  Pallas kernels  145 us (99%)
    pallas_call x1, Pallas kernels, layer(): pl.pallas_call(kernel, out_shape=(jax.ShapeDtypeStruct((IMG, 2 * S, PAT),...  139 us
    pallas_call x1, Pallas kernels, results(): pl.pallas_call(results_kernel, grid=(n,), out_shape=(jax.ShapeDtypeStruct...  5.87 us

profile of v3, /device:TPU:1, one launch (start us, length us, event | category | flops | bytes accessed | tf_op | source)
XLA Modules:
  0.0 145.5 jit_solution(3296128378028553918)
XLA Ops:
  0.6 138.9 %shard_map.102 = (bf16[16,32,128]{2,1,0:T(8,128)(2,1)}, bf16[16,16,1280]{2,1,0:T(8,128)(2,1)}, f32[16,1280]{1,0:T(8,128)}, bf16[1280,640]{1,0:T(8,128)(2,1)}, bf16[640,1280]{1,0:T(8,128)(2,1)}) custom-call(s32[256,1,1280]{2,1,0:T(1,128)} %codes.1, s32[10,1,256]{2,1,0:T(1,128)} %bitcast.10, bf16[2048,1280]{1,0:T(8,128)(2,1)} %bitcast.7, ...), custom_call_target="tpu_custom_call" | custom-call | flops 20999999488 | bytes 40000000 | tf_op jit(solution)/shard_map/pallas_call | solution.py:468
  139.6 5.9 %shard_map.103 = (bf16[16,128,1280]{2,1,0:T(8,128)(2,1)}, f32[16,1280]{1,0:T(8,128)}, bf16[1,1280,640]{2,1,0:T(8,128)(2,1)}, bf16[1,640,1280]{2,1,0:T(8,128)(2,1)}) custom-call(bf16[16,32,128]{2,1,0:T(8,128)(2,1)} %get-tuple-element.13.left, bf16[16,16,1280]{2,1,0:T(8,128)(2,1)} %get-tuple-element.14.bg, bf16[16,1280]{1,0:T(8,128)(2,1)} %bitcast.6, ...), custom_call_target="tpu_custom_call" | custom-call | tf_op jit(solution)/shard_map/pallas_call | solution.py:508

commit v4 on v3

--- a/solution.py
+++ b/solution.py
@@ -225,13 +225,13 @@
 
     cp_win.wait()
     cp_wout.wait()
-    pre(0, 512)
     wait_15(rgr, A2A_G)
     gr_1, gr_2 = row_hops(rgr, GR_HOP)
     for c in gr_1:
         c.start()
+    pre(0, 512)
+    c_wout.start()
     c_win.wait()
-    c_wout.start()
     for c in in_2:
         c.wait_recv()
     pre(0, 0)
@@ -293,8 +293,8 @@
         for t in range(2):
             kp[pl.ds(t * 256, 256), :] = part(act, w, cw, pl.ds(KEEP + t * 256, 256))
 
+    gwo_copy(0).start()
     c_wout.wait()
-    gwo_copy(0).start()
     out_1, out_2 = rs_hops(ps_o, rs_o, h2_o, OUT_RS)
     ig_1, ig_2 = rs_hops(ps_i, rs_i, h2_i, IG_RS)
     send_parts(hid, wout, 0, ps_o, out_1)
@@ -330,7 +330,6 @@
         back[mine_16, :] = fin[pl.ds(pl.multiple_of(eighth(e) * IMG, IMG), IMG), :]
 
     second_hop(out_1, out_2, kp_o, rs_o, h2_o)
-    gwo_copy(1).start()
 
     def fill_gwi(c, carry):
         gwi_s[c] = gwi_dot(1, c).astype(BF16)
@@ -338,7 +337,7 @@
 
     lax.fori_loop(0, 5, fill_gwi, 0)
     second_hop(ig_1, ig_2, kp_i, rs_i, h2_i)
-    for c in range(2, 5):
+    for c in range(1, 5):
         gwo_copy(c).start()
     for c in range(5):
         gwi_copy(c).start()
@@ -368,14 +367,14 @@
     put(fbuf, slice(None), back_o[...].astype(F32))
 
     def tail_comb(c, carry):
-        for k in range(4):
-            i = c * 4 + k
+        for k in range(8):
+            i = c * 8 + k
             cg = dot(every_16th(fbuf, i), go[image(i), :], 1, 1)
             cm = comb[i]
             comb[i] = cm * (cg - jnp.sum(cm * cg, axis=0, keepdims=True))
         return carry
 
-    lax.fori_loop(0, 4, tail_comb, 0)
+    lax.fori_loop(0, 2, tail_comb, 0)
     wait_15(back_i, A2A_I)
     put(gbuf, slice(None), back_i[...].astype(F32))
 
@@ -383,8 +382,8 @@
     cp_bg = here(bgi, bg_out, L_BG)
 
     def tail(c, carry):
-        for k in range(4):
-            i = c * 4 + k
+        for k in range(8):
+            i = c * 8 + k
             bg = every_16th(gbuf, i)
             dg = dot(bg, tok[image(i), :], 1, 1)
             dp = disp[i]
@@ -395,7 +394,7 @@
             bgi[i] = bg
         return carry
 
-    lax.fori_loop(0, 4, tail, 0)
+    lax.fori_loop(0, 2, tail, 0)
     cp_left.start()
     cp_bg.start()
 
@@ -406,7 +405,6 @@
         remote(gp_s.at[dev[1]], gp_r1.at[e], GP_A, dev).start()
     gp_r1[e] = gp_s[e]
 
-    lax.fori_loop(0, 5, finish_gwo, 0)
     wait_many = remote(gp_s.at[pl.ds(0, NE - 1)], gp_r1.at[pl.ds(0, NE - 1)], GP_A, dev_x)
     wait_many.wait()
     total = gp_r1[0]
@@ -416,7 +414,6 @@
     gp_r2[d] = total
     for dev in others_d:
         remote(gp_m.at[0], gp_r2.at[d], GP_B, dev).start()
-    lax.fori_loop(0, 2, finish_gwi, 0)
     wait_many = remote(gp_r2.at[pl.ds(0, ND - 1)], gp_r2.at[pl.ds(0, ND - 1)], GP_B, dev_x)
     wait_many.wait()
     total = gp_r2[0]
@@ -427,7 +424,8 @@
     for dev in others_e:
         remote(gp_m.at[1], gp_f.at[e], GP_C, dev).start()
 
-    lax.fori_loop(2, 5, finish_gwi, 0)
+    lax.fori_loop(0, 5, finish_gwo, 0)
+    lax.fori_loop(0, 5, finish_gwi, 0)
     wait_many = remote(gp_f.at[pl.ds(0, NE - 1)], gp_f.at[pl.ds(0, NE - 1)], GP_C, dev_x)
     wait_many.wait()
     for s in range(S):

time: 146 us -> 144 us (0.986)
  Pallas kernels: 145 us -> 143 us
    pallas_call x1, Pallas kernels: 139 us -> 137 us  [layer(): pl.pallas_call(kernel, out_shape=(jax.ShapeDtypeStruct((IMG, 2 * S, PAT),...]
where the time goes in v4:
time: 144 us
  Pallas kernels  143 us (99%)
    pallas_call x1, Pallas kernels, layer(): pl.pallas_call(kernel, out_shape=(jax.ShapeDtypeStruct((IMG, 2 * S, PAT),...  137 us
    pallas_call x1, Pallas kernels, results(): pl.pallas_call(results_kernel, grid=(n,), out_shape=(jax.ShapeDtypeStruct...  5.87 us

profile of v4, /device:TPU:1, one launch (start us, length us, event | category | flops | bytes accessed | tf_op | source)
XLA Modules:
  0.0 143.6 jit_solution(17665392772683611619)
XLA Ops:
  0.6 137.1 %shard_map.102 = (bf16[16,32,128]{2,1,0:T(8,128)(2,1)}, bf16[16,16,1280]{2,1,0:T(8,128)(2,1)}, f32[16,1280]{1,0:T(8,128)}, bf16[1280,640]{1,0:T(8,128)(2,1)}, bf16[640,1280]{1,0:T(8,128)(2,1)}) custom-call(s32[256,1,1280]{2,1,0:T(1,128)} %codes.1, s32[10,1,256]{2,1,0:T(1,128)} %bitcast.10, bf16[2048,1280]{1,0:T(8,128)(2,1)} %bitcast.7, ...), custom_call_target="tpu_custom_call" | custom-call | flops 20999999488 | bytes 40000000 | tf_op jit(solution)/shard_map/pallas_call | solution.py:466
  137.7 5.9 %shard_map.103 = (bf16[16,128,1280]{2,1,0:T(8,128)(2,1)}, f32[16,1280]{1,0:T(8,128)}, bf16[1,1280,640]{2,1,0:T(8,128)(2,1)}, bf16[1,640,1280]{2,1,0:T(8,128)(2,1)}) custom-call(bf16[16,32,128]{2,1,0:T(8,128)(2,1)} %get-tuple-element.13.left, bf16[16,16,1280]{2,1,0:T(8,128)(2,1)} %get-tuple-element.14.bg, bf16[16,1280]{1,0:T(8,128)(2,1)} %bitcast.6, ...), custom_call_target="tpu_custom_call" | custom-call | tf_op jit(solution)/shard_map/pallas_call | solution.py:506
